TPU v7x, 32 devices: a whole 2x2x4 slice. The times are simulated.
32 devices in a mesh: parts: 2 (over x), lon: 16 (over z, y, core).
Axes of the slice: x: 2, y: 2, z: 4, core: 2. Of those that a mesh axis runs over, the one named last changes fastest.
Arguments:
- solution: float32 [2048, 32, 512], P(('parts', 'lon')), parts along dimension 0, may hold values from -6 to 6
- residual: float32 [2048, 32, 512], P(('parts', 'lon')), parts along dimension 0, may hold values from -12 to 12
- direction: float32 [2048, 32, 512], P(('parts', 'lon')), parts along dimension 0, may hold values from -12 to 12
- land: int32 [2048, 512], P(('parts', 'lon')), parts along dimension 0, may hold values 0 or 1
- clear: int32 [2048, 32, 512], P(('parts', 'lon')), parts along dimension 0, may hold values 0 or 1
- days: int32 [64], P('parts'), parts along dimension 0, may hold values from 0 to 63, as said below
- mixture: float32 [6, 3, 4], P('parts'), parts along dimension 0, may hold values from 0 to 1024, as said below
- q_lon: bfloat16 [1024, 1024], replicated, may hold values from -0.1875 to 0.1875
- q_lat: bfloat16 [512, 512], replicated, may hold values from -0.25 to 0.25
- q_day: bfloat16 [64, 32], P('parts'), parts along dimension 0, may hold values from -1 to 1
- lam_lon: float32 [1024], replicated, may hold values from 0.2 to 5
- lam_lat: float32 [512], replicated, may hold values from 0.2 to 5
- lam_day: float32 [64], P('parts'), parts along dimension 0, may hold values from 0.2 to 5
- noise: float32 [2], P('parts'), parts along dimension 0, may hold values from 0.5 to 2
- rz_mean: float32 [2], P('parts'), parts along dimension 0, may hold values from 0.25 to 1
Outputs:
- new_solution: float32 [2048, 32, 512], P(('parts', 'lon')), parts along dimension 0
- new_residual: float32 [2048, 32, 512], P(('parts', 'lon')), parts along dimension 0
- new_direction: float32 [2048, 32, 512], P(('parts', 'lon')), parts along dimension 0
- new_rz_mean: float32 [2], P('parts'), parts along dimension 0
There are 2 independent parts, one for each index of `parts`. A program takes and returns all parts, laid end to end along the dimension named above; an argument that names none is the same for every part. Nothing has to cross between parts.
Inputs may be any that keep to these rules, and one draw needn't show every extreme that they name: days[k] is 2 k or 2 k + 1, so the days rise strictly within a record of 64 days; the first is 0 and the last 63. mixture[g, 0] are positive weights, mixture[g, 1] frequencies of at most one half per cell or day, mixture[g, 2] positive length scales in cells or days.
All inputs are finite; a program needn't handle non-finite values. No bound on the sum of `land` or of `clear` on one device may be relied on, other than what follows from the above.
Results may differ from a plain program's by a relative error of at most 0.0018.
Values may be sent and summed in bfloat16 or wider, within the bound.
A program may use at most 128 MiB of HBM per device.

v0:
```python
import math
import jax
import jax.numpy as jnp
from jax import lax
from jax.sharding import PartitionSpec as P


def kernel_factor(left, right, params):
    diff = left[:, None] - right[None, :]
    total = jnp.zeros(diff.shape, jnp.float32)
    for comp in range(params.shape[1]):
        weight = params[0, comp]
        freq = params[1, comp]
        length = params[2, comp]
        ratio = diff / length
        total = total + weight * jnp.exp(-0.5 * ratio * ratio) * jnp.cos(
            2.0 * math.pi * freq * diff
        )
    return total.astype(jnp.bfloat16)


def to_exchanged(block):
    flat = block.reshape(block.shape[0], -1)
    return lax.all_to_all(flat, "lon", split_axis=1, concat_axis=0, tiled=True)


def to_longitude(wide, shape):
    back = lax.all_to_all(wide, "lon", split_axis=0, concat_axis=1, tiled=True)
    return back.reshape(shape)


def day_product(matrix, field):
    return jnp.einsum("ck,akb->acb", matrix, field, preferred_element_type=jnp.float32)


def day_product_transposed(matrix, field):
    return jnp.einsum("kc,akb->acb", matrix, field, preferred_element_type=jnp.float32)


def lat_product(matrix, field):
    return jnp.einsum("acj,bj->acb", field, matrix, preferred_element_type=jnp.float32)


def lat_product_transposed(matrix, field):
    return jnp.einsum("acj,jb->acb", field, matrix, preferred_element_type=jnp.float32)


def lon_product_transposed(matrix, wide):
    return lax.dot_general(
        matrix, wide, (((0,), (0,)), ((), ())), preferred_element_type=jnp.float32
    )


def on_device(
    solution,
    residual,
    direction,
    land,
    clear,
    days,
    mixture,
    q_lon,
    q_lat,
    q_day,
    lam_lon,
    lam_lat,
    lam_day,
    noise,
    rz_mean,
):
    bf = jnp.bfloat16
    shape = solution.shape
    lon_dev, n_days, n_lat = shape
    n_lon = q_lon.shape[0]
    cells = n_lon * n_days * n_lat
    observed = (land[:, None, :] * clear).astype(jnp.float32)
    sigma = noise[0]
    lon_pos = jnp.arange(n_lon, dtype=jnp.float32)
    lat_pos = jnp.arange(n_lat, dtype=jnp.float32)
    day_pos = days.astype(jnp.float32)
    k_lon = kernel_factor(lon_pos, lon_pos, mixture[0])
    k_lat = kernel_factor(lat_pos, lat_pos, mixture[1])
    k_day = kernel_factor(day_pos, day_pos, mixture[2])
    first = (observed * direction).astype(bf)
    second = day_product(k_day, first).astype(bf)
    third = lat_product(k_lat, second).astype(bf)
    spread = to_exchanged(third)
    fourth = jnp.dot(k_lon, spread, preferred_element_type=jnp.float32).astype(bf)
    returned = to_longitude(fourth, shape)
    image = observed * (returned.astype(jnp.float32) + sigma * direction)
    curvature = lax.psum(jnp.sum(direction * image), "lon")
    alpha = rz_mean[0] * cells / curvature
    new_solution = solution + alpha * direction
    new_residual = residual - alpha * image
    g_zero = (observed * new_residual).astype(bf)
    g_one = day_product_transposed(q_day, g_zero).astype(bf)
    g_two = lat_product_transposed(q_lat, g_one).astype(bf)
    spread_g = to_exchanged(g_two)
    g_three = lon_product_transposed(q_lon, spread_g).astype(bf)
    g_local = to_longitude(g_three, shape)
    lon_rows = lax.dynamic_slice_in_dim(lam_lon, lax.axis_index("lon") * lon_dev, lon_dev)
    denom = lon_rows[:, None, None] * lam_day[None, :, None] * lam_lat[None, None, :] + sigma
    scaled = (g_local.astype(jnp.float32) / denom).astype(bf)
    spread_h = to_exchanged(scaled)
    h_one = jnp.dot(q_lon, spread_h, preferred_element_type=jnp.float32).astype(bf)
    h_local = to_longitude(h_one, shape)
    h_two = lat_product(q_lat, h_local).astype(bf)
    precond = observed * day_product(q_day, h_two)
    total = lax.psum(jnp.sum(new_residual * precond), "lon")
    new_rz = total / cells
    new_direction = precond + new_rz / rz_mean[0] * direction
    return (new_solution, new_residual, new_direction, new_rz.reshape(1))


def solution(mesh):
    in_specs = (
        P(("parts", "lon"), None, None),
        P(("parts", "lon"), None, None),
        P(("parts", "lon"), None, None),
        P(("parts", "lon"), None),
        P(("parts", "lon"), None, None),
        P("parts"),
        P("parts", None, None),
        P(),
        P(),
        P("parts", None),
        P(),
        P(),
        P("parts"),
        P("parts"),
        P("parts"),
    )
    out_specs = (
        P(("parts", "lon"), None, None),
        P(("parts", "lon"), None, None),
        P(("parts", "lon"), None, None),
        P("parts"),
    )
    return jax.shard_map(
        on_device, mesh=mesh, in_specs=in_specs, out_specs=out_specs, check_vma=False
    )
```

profile of v0, /device:TPU:0, one launch (start us, length us, event | category | flops | bytes accessed | tf_op | source)
XLA Modules:
  0.0 581.4 jit_solution(6673061924529932363)
XLA Ops:
  8.6 31.5 %fusion.50 = bf16[64,32,512]{2,1,0:T(8,128)(2,1)} fusion(f32[64,32,512]{2,1,0:T(8,128)} %param.17, s32[64,32,512]{2,1,0:T(8,128)} %param.19, s32[64,512]{1,0:T(8,128)} %param.18, f32[]{:T(128)} %bitcast.41, f32[]{:T(128)} %bitcast.40, f32[]{:T(128)} %bitcast.39, f32[]{:T(128)} %bitcast.38, f32[]{:T(128)} %bitcast.37, f32[]{:T(128)} %bitcast.36, ...), kind=kOutput, calls=%fused_computation.59 | convolution fusion | flops 1154774016 | bytes 10617056 | tf_op jit(solution)/shard_map/acj,bj->acb/dot_general | solution.py:41
  40.1 4.1 all_to_all.72
  44.1 4.1 copy.32
  48.2 7.4 %all-to-all-start = ((bf16[64,16,1024]{2,0,1:T(8,128)(2,1)}), bf16[64,16,1024]{2,0,1:T(8,128)(2,1)}, u32[]{:S(2)}, u32[]{:S(2)}) async-start(bf16[64,16,1024]{2,0,1:T(8,128)(2,1)} %copy.32), calls=%async_computation | async-start | bytes 4194304 | tf_op jit(solution)/shard_map/all_to_all | solution.py:24
  58.8 38.0 %all-to-all-done = bf16[64,16,1024]{2,0,1:T(8,128)(2,1)} async-done(((bf16[64,16,1024]{2,0,1:T(8,128)(2,1)}), bf16[64,16,1024]{2,0,1:T(8,128)(2,1)}, u32[]{:S(2)}, u32[]{:S(2)}) %all-to-all-start) | async-done | bytes 2097184 | tf_op jit(solution)/shard_map/all_to_all | solution.py:24
  96.8 67.8 %fusion.47 = bf16[1024,1024]{1,0:T(8,128)(2,1)} fusion(bf16[1024,1024]{1,0:T(8,128)(2,1)} %bitcast.44, f32[]{:T(128)} %bitcast.13, f32[]{:T(128)} %bitcast.12, f32[]{:T(128)} %bitcast.11, f32[]{:T(128)} %bitcast.10, f32[]{:T(128)} %bitcast.9, f32[]{:T(128)} %bitcast.8, f32[]{:T(128)} %bitcast.7, f32[]{:T(128)} %bitcast.6, f32[]{:T(128)} %bitcast.5, ...), kind=kOutput, calls=%fused_computation.58 | convolution fusion | flops 2178940928 | bytes 4194352 | tf_op jit(solution)/shard_map/dot_general | solution.py:88
  164.6 11.3 %all-to-all-start.1 = ((bf16[16,64,1024]{2,1,0:T(8,128)(2,1)}), bf16[16,64,1024]{2,1,0:T(8,128)(2,1)}, u32[]{:S(2)}, u32[]{:S(2)}) async-start(bf16[16,64,1024]{2,1,0:T(8,128)(2,1)} %bitcast.121), calls=%async_computation.1 | async-start | bytes 4194304 | tf_op jit(solution)/shard_map/all_to_all | solution.py:28
  177.2 39.9 %all-to-all-done.1 = bf16[16,64,1024]{2,1,0:T(8,128)(2,1)} async-done(((bf16[16,64,1024]{2,1,0:T(8,128)(2,1)}), bf16[16,64,1024]{2,1,0:T(8,128)(2,1)}, u32[]{:S(2)}, u32[]{:S(2)}) %all-to-all-start.1) | async-done | bytes 2097184 | tf_op jit(solution)/shard_map/all_to_all | solution.py:28
  217.1 2.0 convert_bitcast_fusion
  219.1 4.4 copy.33
  223.6 5.0 reshape.116
  228.5 6.9 %multiply_reduce_fusion.1 = f32[]{:T(128)} fusion(f32[64,32,512]{2,1,0:T(8,128)} %param.17, f32[64,32,512]{2,1,0:T(8,128)} %reshape.116, f32[]{:T(128)} %bitcast.114, s32[64,32,512]{2,1,0:T(8,128)} %param.19, s32[64,512]{1,0:T(8,128)S(1)} %copy-done.1), kind=kLoop, calls=%fused_computation.29 | loop fusion | flops 7340031 | bytes 12713992 | tf_op jit(solution)/shard_map/reduce_sum | solution.py:91
  235.4 39.8 %psum.14 = f32[]{:T(128)} all-reduce(f32[]{:T(128)} %multiply_reduce_fusion.1), channel_id=1, replica_groups=mesh['parts'=2,'lon'=16] {'lon'}, use_global_device_ids=true, to_apply=%region_1.0 | all-reduce | flops 1 | bytes 8 | tf_op jit(solution)/shard_map/psum | solution.py:91
  275.9 10.5 %multiply_subtract_fusion = f32[64,32,512]{2,1,0:T(8,128)} fusion(f32[64,32,512]{2,1,0:T(8,128)} %param.16, f32[]{:T(128)S(6)} %div.110, f32[64,32,512]{2,1,0:T(8,128)} %reshape.116, f32[64,32,512]{2,1,0:T(8,128)} %param.17, f32[]{:T(128)} %bitcast.116, s32[64,32,512]{2,1,0:T(8,128)} %param.19, s32[64,512]{1,0:T(8,128)S(1)} %copy-done.1), kind=kLoop, calls=%fused_computation.27 | loop fusion | flops 7340032 | bytes 21102600 | tf_op jit(solution)/shard_map/sub | solution.py:94
  286.4 7.3 %fusion.53 = bf16[64,32,512]{2,1,0:T(8,128)(2,1)} fusion(f32[64,32,512]{2,1,0:T(8,128)} %multiply_subtract_fusion, s32[64,32,512]{2,1,0:T(8,128)} %param.19, s32[64,512]{1,0:T(8,128)S(1)} %copy-done.1, bf16[512,512]{1,0:T(8,128)(2,1)S(1)} %copy-done.2, bf16[32,32]{1,0:T(8,128)(2,1)S(1)} %copy-done.3), kind=kOutput, calls=%fused_computation.60 | convolution fusion | flops 1147142144 | bytes 11143168 | tf_op jit(solution)/shard_map/acj,jb->acb/dot_general | solution.py:45
  293.7 4.1 all_to_all.78
  297.8 2.7 copy.35
  300.5 50.1 %all_to_all.96 = bf16[64,16,1024]{2,0,1:T(8,128)(2,1)S(1)} all-to-all(bf16[64,16,1024]{2,0,1:T(8,128)(2,1)S(1)} %copy.35), channel_id=1, replica_groups=mesh['parts'=2,'lon'=16] {'lon'}, dimensions={1} | all-to-all | bytes 4194304 | tf_op jit(solution)/shard_map/all_to_all | solution.py:24
  350.6 3.7 convolution_convert_fusion.1
  354.4 5.1 all-to-all-start.3
  360.4 2.4 mul.543
  362.7 5.2 mul.544
  367.9 32.7 %all-to-all-done.3 = bf16[16,64,1024]{2,1,0:T(8,128)(2,1)} async-done(((bf16[16,64,1024]{2,1,0:T(8,128)(2,1)}), bf16[16,64,1024]{2,1,0:T(8,128)(2,1)}, u32[]{:S(2)}, u32[]{:S(2)}) %all-to-all-start.3) | async-done | bytes 2097184 | tf_op jit(solution)/shard_map/all_to_all | solution.py:28
  400.7 4.3 fusion.16
  406.2 58.3 %all_to_all.97 = bf16[64,16,1024]{2,0,1:T(8,128)(2,1)S(1)} all-to-all(bf16[64,16,1024]{2,0,1:T(8,128)(2,1)S(1)} %copy.37), channel_id=1, replica_groups=mesh['parts'=2,'lon'=16] {'lon'}, dimensions={1} | all-to-all | bytes 4194304 | tf_op jit(solution)/shard_map/all_to_all | solution.py:24
  464.5 2.4 convolution_convert_fusion
  466.9 52.5 %all_to_all.98 = bf16[16,64,1024]{2,1,0:T(8,128)(2,1)S(1)} all-to-all(bf16[16,64,1024]{2,1,0:T(8,128)(2,1)S(1)} %bitcast.124), channel_id=1, replica_groups=mesh['parts'=2,'lon'=16] {'lon'}, dimensions={0} | all-to-all | bytes 4194304 | tf_op jit(solution)/shard_map/all_to_all | solution.py:28
  519.3 2.5 copy.38
  521.8 4.1 reshape.114
  525.9 9.0 %multiply_reduce_fusion = (f32[]{:T(128)}, f32[64,32,512]{2,1,0:T(8,128)}) fusion(f32[64,32,512]{2,1,0:T(8,128)} %multiply_subtract_fusion, bf16[64,32,512]{2,1,0:T(8,128)(2,1)} %reshape.114, bf16[512,512]{1,0:T(8,128)(2,1)S(1)} %copy-done.2, bf16[32,32]{1,0:T(8,128)(2,1)S(1)} %copy-done.3, s32[64,32,512]{2,1,0:T(8,128)} %param.19, s32[64,512]{1,0:T(8,128)S(1)} %copy-done.1), kind=kOutput, calls=%fused_computation.25 | convolution fusion | flops 1147142144 | bytes 15337476 | tf_op jit(solution)/shard_map/ck,akb->acb/dot_general | solution.py:33
  534.9 33.7 %psum.15 = f32[]{:T(128)} all-reduce(f32[]{:T(128)} %get-tuple-element.45), channel_id=1, replica_groups=mesh['parts'=2,'lon'=16] {'lon'}, use_global_device_ids=true, to_apply=%region_3.0 | all-reduce | flops 1 | bytes 8 | tf_op jit(solution)/shard_map/psum | solution.py:109
  569.3 10.6 %multiply_add_fusion = (f32[64,32,512]{2,1,0:T(8,128)}, f32[64,32,512]{2,1,0:T(8,128)}) fusion(f32[64,32,512]{2,1,0:T(8,128)} %get-tuple-element.46, f32[64,32,512]{2,1,0:T(8,128)} %param.17, f32[]{:T(128)S(6)} %div.113, f32[64,32,512]{2,1,0:T(8,128)} %param.15, f32[]{:T(128)S(6)} %div.110), kind=kLoop, calls=%fused_computation.24 | loop fusion | flops 4194304 | bytes 20971528 | tf_op jit(solution)/shard_map/add | solution.py:111
  (22 shorter events, 5.6 us)
Async XLA Ops:
  0.6 350.0 %copy-start = (bf16[1024,1024]{1,0:T(8,128)(2,1)S(1)}, bf16[1024,1024]{1,0:T(8,128)(2,1)}, u32[]{:S(2)}) copy-start(bf16[1024,1024]{1,0:T(8,128)(2,1)} %param.22) | copy-start | bytes 6291460
  48.2 48.6 %all-to-all-start = ((bf16[64,16,1024]{2,0,1:T(8,128)(2,1)}), bf16[64,16,1024]{2,0,1:T(8,128)(2,1)}, u32[]{:S(2)}, u32[]{:S(2)}) async-start(bf16[64,16,1024]{2,0,1:T(8,128)(2,1)} %copy.32), calls=%async_computation | async-start | bytes 4194304 | tf_op jit(solution)/shard_map/all_to_all | solution.py:24
  164.6 52.4 %all-to-all-start.1 = ((bf16[16,64,1024]{2,1,0:T(8,128)(2,1)}), bf16[16,64,1024]{2,1,0:T(8,128)(2,1)}, u32[]{:S(2)}, u32[]{:S(2)}) async-start(bf16[16,64,1024]{2,1,0:T(8,128)(2,1)} %bitcast.121), calls=%async_computation.1 | async-start | bytes 4194304 | tf_op jit(solution)/shard_map/all_to_all | solution.py:28
  223.6 5.0 copy-start.1
  275.9 10.6 %copy-start.2 = (bf16[512,512]{1,0:T(8,128)(2,1)S(1)}, bf16[512,512]{1,0:T(8,128)(2,1)}, u32[]{:S(2)}) copy-start(bf16[512,512]{1,0:T(8,128)(2,1)} %param.23) | copy-start | bytes 1572868
  275.9 10.5 %copy-start.3 = (bf16[32,32]{1,0:T(8,128)(2,1)S(1)}, bf16[32,32]{1,0:T(8,128)(2,1)}, u32[]{:S(2)}) copy-start(bf16[32,32]{1,0:T(8,128)(2,1)} %param.24) | copy-start | bytes 6148
  354.4 5.1 copy-start.4
  354.4 5.9 %copy-start.5 = (f32[32]{0:T(128)S(1)}, f32[32]{0:T(128)}, u32[]{:S(2)}) copy-start(f32[32]{0:T(128)} %param.27) | copy-start | bytes 388
  354.4 46.3 %all-to-all-start.3 = ((bf16[16,64,1024]{2,1,0:T(8,128)(2,1)}), bf16[16,64,1024]{2,1,0:T(8,128)(2,1)}, u32[]{:S(2)}, u32[]{:S(2)}) async-start(bf16[16,64,1024]{2,1,0:T(8,128)(2,1)} %bitcast.120), calls=%async_computation.3 | async-start | bytes 4194304 | tf_op jit(solution)/shard_map/all_to_all | solution.py:28
where the time goes:
time: 591 us; the launch traced here: 581 us
  blocking collectives  234 us (40%)
  matrix products  122 us (21%)
  waiting for transfers between devices  111 us (19%)
  local copies, waits for them, and re-layouts  43.2 us (7%)
  other arithmetic  35.3 us (6%)
  starting transfers between devices  23.8 us (4%)
  between operations  12.5 us (2%)
    all_to_all x2, blocking collectives, to_exchanged(): return lax.all_to_all(flat, 'lon', split_axis=1, concat_axis=0, tiled=True)  108 us
    all_to_all x2, waiting for transfers between devices, to_longitude(): back = lax.all_to_all(wide, 'lon', split_axis=0, concat_axis=1, tiled=True)  72.6 us
    dot_general x1, matrix products, on_device(): jnp.dot(k_lon, spread, preferred_element_type=jnp.float32).astype(bf)  67.8 us
    all_to_all x1, blocking collectives, to_longitude(): back = lax.all_to_all(wide, 'lon', split_axis=0, concat_axis=1, tiled=True)  52.5 us
    psum x1, blocking collectives, on_device(): curvature = lax.psum(jnp.sum(direction * image), 'lon')  39.8 us
    all_to_all x1, waiting for transfers between devices, to_exchanged(): return lax.all_to_all(flat, 'lon', split_axis=1, concat_axis=0, tiled=True)  38 us
    psum x1, blocking collectives, on_device(): total = lax.psum(jnp.sum(new_residual * precond), 'lon')  33.7 us
    dot_general x1, matrix products, lat_product(): jnp.einsum('acj,bj->acb', field, matrix, preferred_element_type=jnp.float32)  31.5 us
  transfers between devices with their start and end apart: 3, of which 3 were waited for; matrix products, arithmetic and copies ran while one was open for 2% of the time, Pallas kernels for 0%

commit v1 on v0

--- a/solution.py
+++ b/solution.py
@@ -3,6 +3,13 @@
 import jax.numpy as jnp
 from jax import lax
 from jax.sharding import PartitionSpec as P
+
+
+def exchange_blocks(x, name, split, join):
+    size = lax.axis_size(name)
+    blocks = jnp.stack(jnp.split(x, size, axis=split), axis=0)
+    blocks = lax.all_to_all(blocks, name, split_axis=0, concat_axis=0)
+    return jnp.concatenate(blocks, axis=join)
 
 
 def kernel_factor(left, right, params):
@@ -25,7 +32,7 @@
 
 
 def to_longitude(wide, shape):
-    back = lax.all_to_all(wide, "lon", split_axis=0, concat_axis=1, tiled=True)
+    back = exchange_blocks(wide, "lon", 0, 1)
     return back.reshape(shape)
 
 

time: 591 us -> 611 us (1.034)
  local copies, waits for them, and re-layouts: 43.2 us -> 63.4 us
    unnamed x14 -> x59, local copies, waits for them, and re-layouts: 0.04 us -> 20.1 us
where the time goes in v1:
time: 611 us; the launch traced here: 601 us
  blocking collectives  234 us (38%)
  matrix products  120 us (20%)
  waiting for transfers between devices  111 us (18%)
  local copies, waits for them, and re-layouts  63.4 us (10%)
  other arithmetic  36.3 us (6%)
  starting transfers between devices  23.8 us (4%)
  between operations  12.6 us (2%)
    all_to_all x2, blocking collectives, to_exchanged(): return lax.all_to_all(flat, 'lon', split_axis=1, concat_axis=0, tiled=True)  108 us
    all_to_all x2, waiting for transfers between devices, exchange_blocks(): blocks = lax.all_to_all(blocks, name, split_axis=0, concat_axis=0)  72.6 us
    dot_general x1, matrix products, on_device(): jnp.dot(k_lon, spread, preferred_element_type=jnp.float32).astype(bf)  67 us
    all_to_all x1, blocking collectives, exchange_blocks(): blocks = lax.all_to_all(blocks, name, split_axis=0, concat_axis=0)  52.5 us
    psum x1, blocking collectives, on_device(): curvature = lax.psum(jnp.sum(direction * image), 'lon')  39.8 us
    all_to_all x1, waiting for transfers between devices, to_exchanged(): return lax.all_to_all(flat, 'lon', split_axis=1, concat_axis=0, tiled=True)  38 us
    psum x1, blocking collectives, on_device(): total = lax.psum(jnp.sum(new_residual * precond), 'lon')  33.7 us
    dot_general x1, matrix products, lat_product(): jnp.einsum('acj,bj->acb', field, matrix, preferred_element_type=jnp.float32)  31.5 us
  transfers between devices with their start and end apart: 3, of which 3 were waited for; matrix products, arithmetic and copies ran while one was open for 2% of the time, Pallas kernels for 0%

profile of v1, /device:TPU:0, one launch (start us, length us, event | category | flops | bytes accessed | tf_op | source)
XLA Modules:
  0.0 600.7 jit_solution(3457881618662303230)
XLA Ops:
  8.6 31.5 %fusion.51 = bf16[64,32,512]{2,1,0:T(8,128)(2,1)} fusion(f32[64,32,512]{2,1,0:T(8,128)} %param.17, s32[64,32,512]{2,1,0:T(8,128)} %param.19, s32[64,512]{1,0:T(8,128)} %param.18, f32[]{:T(128)} %bitcast.41, f32[]{:T(128)} %bitcast.40, f32[]{:T(128)} %bitcast.39, f32[]{:T(128)} %bitcast.38, f32[]{:T(128)} %bitcast.37, f32[]{:T(128)} %bitcast.36, ...), kind=kOutput, calls=%fused_computation.63 | convolution fusion | flops 1154774016 | bytes 10617056 | tf_op jit(solution)/shard_map/acj,bj->acb/dot_general | solution.py:48
  40.1 4.1 all_to_all.49
  44.1 4.1 copy.19
  48.2 7.4 %all-to-all-start = ((bf16[64,16,1024]{2,0,1:T(8,128)(2,1)}), bf16[64,16,1024]{2,0,1:T(8,128)(2,1)}, u32[]{:S(2)}, u32[]{:S(2)}) async-start(bf16[64,16,1024]{2,0,1:T(8,128)(2,1)} %copy.19), calls=%async_computation | async-start | bytes 4194304 | tf_op jit(solution)/shard_map/all_to_all | solution.py:31
  58.8 38.0 %all-to-all-done = bf16[64,16,1024]{2,0,1:T(8,128)(2,1)} async-done(((bf16[64,16,1024]{2,0,1:T(8,128)(2,1)}), bf16[64,16,1024]{2,0,1:T(8,128)(2,1)}, u32[]{:S(2)}, u32[]{:S(2)}) %all-to-all-start) | async-done | bytes 2097184 | tf_op jit(solution)/shard_map/all_to_all | solution.py:31
  96.8 67.0 %fusion.48 = bf16[1024,1024]{1,0:T(8,128)(2,1)S(1)} fusion(bf16[1024,1024]{1,0:T(8,128)(2,1)} %bitcast.44, f32[]{:T(128)} %bitcast.13, f32[]{:T(128)} %bitcast.12, f32[]{:T(128)} %bitcast.11, f32[]{:T(128)} %bitcast.10, f32[]{:T(128)} %bitcast.9, f32[]{:T(128)} %bitcast.8, f32[]{:T(128)} %bitcast.7, f32[]{:T(128)} %bitcast.6, f32[]{:T(128)} %bitcast.5, ...), kind=kOutput, calls=%fused_computation.62 | convolution fusion | flops 2178940928 | bytes 4194352 | tf_op jit(solution)/shard_map/dot_general | solution.py:95
  174.5 11.3 %all-to-all-start.1 = ((bf16[16,64,1024]{2,1,0:T(8,128)(2,1)}), bf16[16,64,1024]{2,1,0:T(8,128)(2,1)}, u32[]{:S(2)}, u32[]{:S(2)}) async-start(bf16[16,64,1024]{2,1,0:T(8,128)(2,1)} %fusion.123), calls=%async_computation.1 | async-start | bytes 4194304 | tf_op jit(solution)/shard_map/all_to_all | solution.py:11
  187.0 39.9 %all-to-all-done.1 = bf16[16,64,1024]{2,1,0:T(8,128)(2,1)} async-done(((bf16[16,64,1024]{2,1,0:T(8,128)(2,1)}), bf16[16,64,1024]{2,1,0:T(8,128)(2,1)}, u32[]{:S(2)}, u32[]{:S(2)}) %all-to-all-start.1) | async-done | bytes 2097184 | tf_op jit(solution)/shard_map/all_to_all | solution.py:11
  226.9 2.0 convert_bitcast_fusion
  229.0 4.4 copy.20
  233.4 5.0 reshape.104
  238.4 6.9 %multiply_reduce_fusion.1 = f32[]{:T(128)} fusion(f32[64,32,512]{2,1,0:T(8,128)} %param.17, f32[64,32,512]{2,1,0:T(8,128)} %reshape.104, f32[]{:T(128)} %bitcast.302, s32[64,32,512]{2,1,0:T(8,128)} %param.19, s32[64,512]{1,0:T(8,128)S(1)} %copy-done.1), kind=kLoop, calls=%fused_computation.31 | loop fusion | flops 7340031 | bytes 12713992 | tf_op jit(solution)/shard_map/reduce_sum | solution.py:98
  245.2 39.8 %psum.14 = f32[]{:T(128)} all-reduce(f32[]{:T(128)} %multiply_reduce_fusion.1), channel_id=1, replica_groups=mesh['parts'=2,'lon'=16] {'lon'}, use_global_device_ids=true, to_apply=%region_1.0 | all-reduce | flops 1 | bytes 8 | tf_op jit(solution)/shard_map/psum | solution.py:98
  285.8 10.5 %multiply_subtract_fusion = f32[64,32,512]{2,1,0:T(8,128)} fusion(f32[64,32,512]{2,1,0:T(8,128)} %param.16, f32[]{:T(128)S(6)} %div.110, f32[64,32,512]{2,1,0:T(8,128)} %reshape.104, f32[64,32,512]{2,1,0:T(8,128)} %param.17, f32[]{:T(128)} %bitcast.304, s32[64,32,512]{2,1,0:T(8,128)} %param.19, s32[64,512]{1,0:T(8,128)S(1)} %copy-done.1), kind=kLoop, calls=%fused_computation.29 | loop fusion | flops 7340032 | bytes 21102600 | tf_op jit(solution)/shard_map/sub | solution.py:101
  296.3 7.3 %fusion.54 = bf16[64,32,512]{2,1,0:T(8,128)(2,1)} fusion(f32[64,32,512]{2,1,0:T(8,128)} %multiply_subtract_fusion, s32[64,32,512]{2,1,0:T(8,128)} %param.19, s32[64,512]{1,0:T(8,128)S(1)} %copy-done.1, bf16[512,512]{1,0:T(8,128)(2,1)S(1)} %copy-done.2, bf16[32,32]{1,0:T(8,128)(2,1)S(1)} %copy-done.3), kind=kOutput, calls=%fused_computation.64 | convolution fusion | flops 1147142144 | bytes 11143168 | tf_op jit(solution)/shard_map/acj,jb->acb/dot_general | solution.py:52
  303.6 4.1 all_to_all.54
  307.6 2.7 copy.21
  310.4 50.1 %all_to_all.69 = bf16[64,16,1024]{2,0,1:T(8,128)(2,1)S(1)} all-to-all(bf16[64,16,1024]{2,0,1:T(8,128)(2,1)S(1)} %copy.21), channel_id=1, replica_groups=mesh['parts'=2,'lon'=16] {'lon'}, dimensions={1} | all-to-all | bytes 4194304 | tf_op jit(solution)/shard_map/all_to_all | solution.py:31
  360.5 2.4 convert_bitcast_fusion.2
  373.5 5.1 all-to-all-start.3
  379.5 2.4 mul.543
  381.8 5.2 mul.544
  387.1 32.7 %all-to-all-done.3 = bf16[16,64,1024]{2,1,0:T(8,128)(2,1)} async-done(((bf16[16,64,1024]{2,1,0:T(8,128)(2,1)}), bf16[16,64,1024]{2,1,0:T(8,128)(2,1)}, u32[]{:S(2)}, u32[]{:S(2)}) %all-to-all-start.3) | async-done | bytes 2097184 | tf_op jit(solution)/shard_map/all_to_all | solution.py:11
  419.8 5.3 fusion.16
  425.1 58.3 %all_to_all.70 = bf16[64,16,1024]{2,0,1:T(8,128)(2,1)S(1)} all-to-all(bf16[64,16,1024]{2,0,1:T(8,128)(2,1)S(1)} %fusion.16), channel_id=1, replica_groups=mesh['parts'=2,'lon'=16] {'lon'}, dimensions={1} | all-to-all | bytes 4194304 | tf_op jit(solution)/shard_map/all_to_all | solution.py:31
  483.4 2.4 convert_bitcast_fusion.1
  486.1 52.5 %all_to_all.71 = bf16[16,64,1024]{2,1,0:T(8,128)(2,1)S(1)} all-to-all(bf16[16,64,1024]{2,1,0:T(8,128)(2,1)S(1)} %fusion.91), channel_id=1, replica_groups=mesh['parts'=2,'lon'=16] {'lon'}, dimensions={0} | all-to-all | bytes 4194304 | tf_op jit(solution)/shard_map/all_to_all | solution.py:11
  538.6 2.5 copy.23
  541.1 4.1 reshape_reshape.2
  545.1 9.0 %multiply_reduce_fusion = (f32[]{:T(128)}, f32[64,32,512]{2,1,0:T(8,128)}) fusion(f32[64,32,512]{2,1,0:T(8,128)} %multiply_subtract_fusion, bf16[64,32,512]{2,1,0:T(8,128)(2,1)} %reshape_reshape.2, bf16[512,512]{1,0:T(8,128)(2,1)S(1)} %copy-done.2, bf16[32,32]{1,0:T(8,128)(2,1)S(1)} %copy-done.3, s32[64,32,512]{2,1,0:T(8,128)} %param.19, ...), kind=kOutput, calls=%fused_computation.27 | convolution fusion | flops 1147142144 | bytes 15337476 | tf_op jit(solution)/shard_map/ck,akb->acb/dot_general | solution.py:40
  554.1 33.7 %psum.15 = f32[]{:T(128)} all-reduce(f32[]{:T(128)} %get-tuple-element.45), channel_id=1, replica_groups=mesh['parts'=2,'lon'=16] {'lon'}, use_global_device_ids=true, to_apply=%region_3.0 | all-reduce | flops 1 | bytes 8 | tf_op jit(solution)/shard_map/psum | solution.py:116
  588.5 10.6 %multiply_add_fusion = (f32[64,32,512]{2,1,0:T(8,128)}, f32[64,32,512]{2,1,0:T(8,128)}) fusion(f32[64,32,512]{2,1,0:T(8,128)} %get-tuple-element.46, f32[64,32,512]{2,1,0:T(8,128)} %param.17, f32[]{:T(128)S(6)} %div.113, f32[64,32,512]{2,1,0:T(8,128)} %param.15, f32[]{:T(128)S(6)} %div.110), kind=kLoop, calls=%fused_computation.26 | loop fusion | flops 4194304 | bytes 20971528 | tf_op jit(solution)/shard_map/add | solution.py:118
  (69 shorter events, 25.8 us)
Async XLA Ops:
  0.6 359.9 %copy-start = (bf16[1024,1024]{1,0:T(8,128)(2,1)S(1)}, bf16[1024,1024]{1,0:T(8,128)(2,1)}, u32[]{:S(2)}) copy-start(bf16[1024,1024]{1,0:T(8,128)(2,1)} %param.22) | copy-start | bytes 6291460
  48.2 48.6 %all-to-all-start = ((bf16[64,16,1024]{2,0,1:T(8,128)(2,1)}), bf16[64,16,1024]{2,0,1:T(8,128)(2,1)}, u32[]{:S(2)}, u32[]{:S(2)}) async-start(bf16[64,16,1024]{2,0,1:T(8,128)(2,1)} %copy.19), calls=%async_computation | async-start | bytes 4194304 | tf_op jit(solution)/shard_map/all_to_all | solution.py:31
  174.5 52.4 %all-to-all-start.1 = ((bf16[16,64,1024]{2,1,0:T(8,128)(2,1)}), bf16[16,64,1024]{2,1,0:T(8,128)(2,1)}, u32[]{:S(2)}, u32[]{:S(2)}) async-start(bf16[16,64,1024]{2,1,0:T(8,128)(2,1)} %fusion.123), calls=%async_computation.1 | async-start | bytes 4194304 | tf_op jit(solution)/shard_map/all_to_all | solution.py:11
  233.4 5.0 copy-start.1
  285.7 10.6 %copy-start.2 = (bf16[512,512]{1,0:T(8,128)(2,1)S(1)}, bf16[512,512]{1,0:T(8,128)(2,1)}, u32[]{:S(2)}) copy-start(bf16[512,512]{1,0:T(8,128)(2,1)} %param.23) | copy-start | bytes 1572868
  285.8 10.5 %copy-start.3 = (bf16[32,32]{1,0:T(8,128)(2,1)S(1)}, bf16[32,32]{1,0:T(8,128)(2,1)}, u32[]{:S(2)}) copy-start(bf16[32,32]{1,0:T(8,128)(2,1)} %param.24) | copy-start | bytes 6148
  373.5 5.1 copy-start.4
  373.5 5.9 copy-start.5
  373.5 46.3 %all-to-all-start.3 = ((bf16[16,64,1024]{2,1,0:T(8,128)(2,1)}), bf16[16,64,1024]{2,1,0:T(8,128)(2,1)}, u32[]{:S(2)}, u32[]{:S(2)}) async-start(bf16[16,64,1024]{2,1,0:T(8,128)(2,1)} %fusion.107), calls=%async_computation.3 | async-start | bytes 4194304 | tf_op jit(solution)/shard_map/all_to_all | solution.py:11
